TPU v7x, 256 devices: a whole 4x4x8 slice. The times are simulated.
256 devices in a mesh: ctx: 32 (over z, y), ch: 8 (over x, core).
Axes of the slice: x: 4, y: 4, z: 8, core: 2. Of those that a mesh axis runs over, the one named last changes fastest.
Arguments:
- queries: bfloat16 [8192, 4096], P('ctx', 'ch'), may hold values from -6 to 6
- keys: bfloat16 [8192, 4096], P('ctx', 'ch'), may hold values from -6 to 6
- values: bfloat16 [8192, 4096], P('ctx', 'ch'), may hold values from -6 to 6
- long_filter: float32 [8192, 4096], P('ctx', 'ch'), may hold values from -1.05 to 1.05
- short_filters: float32 [3, 3, 4096], P(None, None, 'ch'), may hold values from -3.6 to 3.6
- skip: float32 [4096], P('ch'), may hold values from -1 to 1
- w_out: bfloat16 [4096, 8192], P('ch'), may hold values from -0.09375 to 0.09375
- d_out: bfloat16 [8192, 8192], P('ctx', 'ch'), may hold values from -6 to 6
Outputs:
- d_queries: bfloat16 [8192, 4096], P('ctx', 'ch')
- d_keys: bfloat16 [8192, 4096], P('ctx', 'ch')
- d_values: bfloat16 [8192, 4096], P('ctx', 'ch')
- d_long: float32 [8192, 4096], P('ctx', 'ch')
- d_short: float32 [3, 3, 4096], P(None, None, 'ch')
- d_skip: float32 [4096], P('ch')
All inputs are finite; a program needn't handle non-finite values.
Results may differ from a plain program's by a relative error of at most 0.0049.
Values may be sent and summed in bfloat16 or wider, within the bound.
No kernel may reach another device: no remote copies, remote signals or barrier semaphores. Data moves between devices by JAX's collectives and lax.ppermute only.
A program may use at most 128 MiB of HBM per device.

v0:
```python
import math
import jax
import jax.numpy as jnp
from jax import lax
from jax.sharding import PartitionSpec as P


def passed_along(block, axis, distance):
    devices = range(lax.axis_size(axis))
    route = [(i - distance, i) for i in devices if i - distance in devices]
    return lax.ppermute(block, axis, route)


def phases(left_index, right_index, modulus):
    product = left_index[:, None] * right_index[None, :] % modulus
    angle = product.astype(jnp.float32) * (2.0 * math.pi / modulus)
    return (jnp.cos(angle), jnp.sin(angle))


def mat_apply(table, data, form):
    return jnp.einsum(form, table, data, precision=lax.Precision.HIGHEST)


def forward_full(regrouped, ctx_size, position, block_len, total_len):
    seq_rows = ctx_size * block_len
    coarse = jnp.arange(ctx_size, dtype=jnp.int32)
    freq_coarse = jnp.arange(2 * ctx_size, dtype=jnp.int32)
    coarse_cos, coarse_sin = phases(freq_coarse, coarse, 2 * ctx_size)
    first_real = mat_apply(coarse_cos, regrouped, "ka,sabc->skbc")
    first_imag = -mat_apply(coarse_sin, regrouped, "ka,sabc->skbc")
    fine_global = position * block_len + jnp.arange(block_len, dtype=jnp.int32)
    twist_cos, twist_sin = phases(freq_coarse, fine_global, total_len)
    twist_cos = twist_cos[None, :, :, None]
    twist_sin = twist_sin[None, :, :, None]
    second_real = first_real * twist_cos + first_imag * twist_sin
    second_imag = first_imag * twist_cos - first_real * twist_sin
    moved = lax.all_to_all(
        jnp.stack([second_real, second_imag], axis=1),
        "ctx",
        split_axis=2,
        concat_axis=3,
        tiled=True,
    )
    fine_index = jnp.arange(seq_rows, dtype=jnp.int32)
    fine_cos, fine_sin = phases(fine_index, fine_index, seq_rows)
    moved_real = moved[:, 0]
    moved_imag = moved[:, 1]
    spec_real = mat_apply(fine_cos, moved_real, "kb,smbc->smkc") + mat_apply(
        fine_sin, moved_imag, "kb,smbc->smkc"
    )
    spec_imag = mat_apply(fine_cos, moved_imag, "kb,smbc->smkc") - mat_apply(
        fine_sin, moved_real, "kb,smbc->smkc"
    )
    return (spec_real, spec_imag)


def inverse_full(spec_real, spec_imag, ctx_size, position, block_len, total_len):
    seq_rows = spec_real.shape[2]
    fine_index = jnp.arange(seq_rows, dtype=jnp.int32)
    fine_cos, fine_sin = phases(fine_index, fine_index, seq_rows)
    back_real = mat_apply(fine_cos, spec_real, "bk,smkc->smbc") - mat_apply(
        fine_sin, spec_imag, "bk,smkc->smbc"
    )
    back_imag = mat_apply(fine_cos, spec_imag, "bk,smkc->smbc") + mat_apply(
        fine_sin, spec_real, "bk,smkc->smbc"
    )
    returned = lax.all_to_all(
        jnp.stack([back_real, back_imag], axis=1), "ctx", split_axis=3, concat_axis=2, tiled=True
    )
    part_real = returned[:, 0]
    part_imag = returned[:, 1]
    freq_coarse = jnp.arange(2 * ctx_size, dtype=jnp.int32)
    fine_global = position * block_len + jnp.arange(block_len, dtype=jnp.int32)
    twist_cos, twist_sin = phases(freq_coarse, fine_global, total_len)
    twist_cos = twist_cos[None, :, :, None]
    twist_sin = twist_sin[None, :, :, None]
    turned_real = part_real * twist_cos - part_imag * twist_sin
    turned_imag = part_imag * twist_cos + part_real * twist_sin
    coarse = jnp.arange(ctx_size, dtype=jnp.int32)
    coarse_cos, coarse_sin = phases(coarse, freq_coarse, 2 * ctx_size)
    result_real = mat_apply(coarse_cos, turned_real, "ak,skbc->sabc") - mat_apply(
        coarse_sin, turned_imag, "ak,skbc->sabc"
    )
    result_imag = mat_apply(coarse_cos, turned_imag, "ak,skbc->sabc") + mat_apply(
        coarse_sin, turned_real, "ak,skbc->sabc"
    )
    return (result_real / total_len, result_imag / total_len)


def per_device(queries, keys, values, long_filter, short_filters, skip, w_out, d_out):
    ctx_size = lax.axis_size("ctx")
    position = lax.axis_index("ctx")
    seq_rows = queries.shape[0]
    width = queries.shape[1]
    block_len = seq_rows // ctx_size
    total_len = 2 * ctx_size * seq_rows
    tap_count = short_filters.shape[1]
    rim_width = tap_count - 1
    streams = jnp.stack([queries, keys, values])
    before = passed_along(streams[:, seq_rows - rim_width :, :], "ctx", 1)
    extended = jnp.concatenate([before, streams], axis=1).astype(jnp.float32)
    filtered = jnp.zeros((3, seq_rows, width), jnp.float32)
    for j in range(tap_count):
        filtered = (
            filtered
            + short_filters[:, j, None, :]
            * extended[:, rim_width - j : rim_width - j + seq_rows, :]
        )
    mixed = filtered[1] * filtered[2]
    accumulated = lax.dot_general(
        lax.all_gather(d_out, "ch", axis=1, tiled=True),
        w_out,
        (((1,), (1,)), ((), ())),
        preferred_element_type=jnp.float32,
    )
    grad_o = lax.optimization_barrier(accumulated.astype(jnp.bfloat16)).astype(jnp.float32)
    grad_y = grad_o * filtered[0]
    signals = jnp.stack([mixed, long_filter, grad_y])
    regrouped = lax.all_to_all(signals[:, None], "ctx", split_axis=2, concat_axis=1, tiled=True)
    spec_real, spec_imag = forward_full(regrouped, ctx_size, position, block_len, total_len)
    mix_re, mix_im = (spec_real[0], spec_imag[0])
    fil_re, fil_im = (spec_real[1], spec_imag[1])
    grad_re, grad_im = (spec_real[2], spec_imag[2])
    out_re = mix_re * fil_re - mix_im * fil_im
    out_im = mix_re * fil_im + mix_im * fil_re
    back_re = grad_re * fil_re + grad_im * fil_im
    back_im = grad_im * fil_re - grad_re * fil_im
    corr_re = grad_re * mix_re + grad_im * mix_im
    corr_im = grad_im * mix_re - grad_re * mix_im
    result_real, result_imag = inverse_full(
        jnp.stack([out_re, back_re, corr_re]),
        jnp.stack([out_im, back_im, corr_im]),
        ctx_size,
        position,
        block_len,
        total_len,
    )
    timed = lax.all_to_all(result_real, "ctx", split_axis=1, concat_axis=2, tiled=True).reshape(
        3, seq_rows, width
    )
    conv_y = timed[0]
    conv_back = timed[1]
    d_long = timed[2]
    y_full = conv_y + skip[None, :] * mixed
    grad_mixed = conv_back + skip[None, :] * grad_y
    grads = jnp.stack([grad_o * y_full, grad_mixed * filtered[2], grad_mixed * filtered[1]])
    after = passed_along(grads[:, :rim_width, :], "ctx", -1)
    grads_ext = jnp.concatenate([grads, after], axis=1)
    stream_grads = jnp.zeros((3, seq_rows, width), jnp.float32)
    tap_terms = []
    for j in range(tap_count):
        stream_grads = (
            stream_grads + short_filters[:, j, None, :] * grads_ext[:, j : j + seq_rows, :]
        )
        tap_terms.append(
            jnp.sum(grads * extended[:, rim_width - j : rim_width - j + seq_rows, :], axis=1)
        )
    short_terms = jnp.stack(tap_terms, axis=1)
    skip_term = jnp.sum(grad_y * mixed, axis=0)
    d_short, d_skip = lax.psum((short_terms, skip_term), "ctx")
    return (
        stream_grads[0].astype(jnp.bfloat16),
        stream_grads[1].astype(jnp.bfloat16),
        stream_grads[2].astype(jnp.bfloat16),
        d_long,
        d_short,
        d_skip,
    )


def solution(mesh):
    in_specs = (
        P("ctx", "ch"),
        P("ctx", "ch"),
        P("ctx", "ch"),
        P("ctx", "ch"),
        P(None, None, "ch"),
        P("ch"),
        P("ch", None),
        P("ctx", "ch"),
    )
    out_specs = (
        P("ctx", "ch"),
        P("ctx", "ch"),
        P("ctx", "ch"),
        P("ctx", "ch"),
        P(None, None, "ch"),
        P("ch"),
    )
    return jax.shard_map(
        per_device, mesh=mesh, in_specs=in_specs, out_specs=out_specs, check_vma=False
    )
```

profile of v0, /device:TPU:128, one launch (start us, length us, event | category | flops | bytes accessed | tf_op | source)
XLA Modules:
  0.0 701.8 jit_solution(1200529167491770491)
XLA Ops:
  13.0 4.5 collective-permute-done
  20.2 25.8 %all-gather.2.cloned.1.call-done = bf16[256,8192]{1,0:T(8,128)(2,1)} async-done(((bf16[256,1024]{1,0:T(8,128)(2,1)}), bf16[256,8192]{1,0:T(8,128)(2,1)}) %all-gather.2.cloned.1.call-update) | async-done | bytes 4194320 | tf_op jit(solution)/shard_map/all_gather | solution.py:111
  46.0 7.1 %convolution_convert_fusion = bf16[256,512]{1,0:T(8,128)(2,1)S(1)} fusion(bf16[256,8192]{1,0:T(8,128)(2,1)} %all-gather.2.cloned.1.call-done, bf16[512,8192]{1,0:T(8,128)(2,1)} %param.14), kind=kOutput, calls=%fused_computation.60 | convolution fusion | flops 2147614720 | bytes 12845056 | tf_op jit(solution)/shard_map/dot_general | solution.py:110
  56.1 10.0 %all-to-all-start = ((f32[3,1,256,512]{3,1,0,2:T(1,128)}), f32[3,1,256,512]{3,1,0,2:T(1,128)}, u32[]{:S(2)}, u32[]{:S(2)}) async-start(f32[3,1,256,512]{3,1,0,2:T(1,128)} %copy.56), calls=%async_computation | async-start | bytes 3145728 | tf_op jit(solution)/shard_map/all_to_all | solution.py:119
  66.3 36.3 %all-to-all-done = f32[3,1,256,512]{3,1,0,2:T(1,128)} async-done(((f32[3,1,256,512]{3,1,0,2:T(1,128)}), f32[3,1,256,512]{3,1,0,2:T(1,128)}, u32[]{:S(2)}, u32[]{:S(2)}) %all-to-all-start) | async-done | bytes 1572896 | tf_op jit(solution)/shard_map/all_to_all | solution.py:119
  104.2 4.0 fusion.29
  108.1 4.9 fusion.1
  114.3 4.0 copy.60
  118.4 145.3 %all_to_all.57 = f32[3,2,64,8,512]{4,3,0,1,2:T(8,128)S(1)} all-to-all(f32[3,2,64,8,512]{4,3,0,1,2:T(8,128)S(1)} %copy.60), channel_id=1, replica_groups=mesh['ctx'=32,'ch'=8] {'ctx'}, dimensions={2} | all-to-all | bytes 12582912 | tf_op jit(solution)/shard_map/all_to_all | solution.py:37
  264.8 6.3 fusion.12
  271.1 6.5 fusion.13
  277.5 6.4 subtract_bitcast_fusion.1
  284.0 6.7 add_bitcast_fusion.1
  298.9 4.0 subtract_bitcast_fusion
  310.3 10.3 %copy.65 = f32[3,2,2,256,512]{4,2,0,1,3:T(2,128)} copy(f32[3,2,2,256,512]{3,4,2,0,1:T(8,128)} %pad_maximum_fusion.1) | data formatting | bytes 12582912 | tf_op jit(solution)/shard_map/stack | solution.py:68
  320.6 144.6 %all_to_all.58 = f32[3,2,2,256,512]{4,2,0,1,3:T(2,128)S(1)} all-to-all(f32[3,2,2,256,512]{4,2,0,1,3:T(2,128)} %copy.65), channel_id=1, replica_groups=mesh['ctx'=32,'ch'=8] {'ctx'}, dimensions={3} | all-to-all | bytes 12582912 | tf_op jit(solution)/shard_map/all_to_all | solution.py:67
  465.2 4.6 copy.97
  469.8 10.3 %copy.67 = f32[3,2,32,2,8,512]{5,3,2,4,0,1:T(2,128)} copy(f32[3,2,32,2,8,512]{5,4,2,3,1,0:T(8,128)} %bitcast.217) | data formatting | bytes 12582912 | tf_op jit(solution)/shard_map/all_to_all | solution.py:67
  480.1 8.5 %all_to_all.51 = f32[3,2,64,8,512]{4,2,3,0,1:T(8,128)} reshape(f32[3,2,32,2,8,512]{5,3,2,4,0,1:T(2,128)} %copy.67) | data formatting | bytes 12582912 | tf_op jit(solution)/shard_map/all_to_all | solution.py:67
  488.6 4.5 fusion.4
  493.1 4.6 multiply_bitcast_fusion
  498.6 43.2 %all_to_all.59 = f32[3,32,8,512]{3,2,0,1:T(8,128)S(1)} all-to-all(f32[3,32,8,512]{3,2,0,1:T(8,128)S(1)} %copy.68), channel_id=1, replica_groups=mesh['ctx'=32,'ch'=8] {'ctx'}, dimensions={1} | all-to-all | bytes 3145728 | tf_op jit(solution)/shard_map/all_to_all | solution.py:138
  542.3 4.9 collective-permute-start.1
  549.9 143.3 %all-reduce = (f32[3,3,512]{2,0,1:T(4,128)S(1)}, f32[512]{0:T(512)}) all-reduce(f32[3,3,512]{2,0,1:T(4,128)S(1)} %pad_maximum_fusion.14, f32[512]{0:T(512)S(1)} %get-tuple-element.46), channel_id=1, replica_groups=mesh['ctx'=32,'ch'=8] {'ctx'}, use_global_device_ids=true, to_apply=%region_3.4 | all-reduce | flops 5120 | bytes 40960 | tf_op jit(solution)/shard_map/psum | solution.py:160
  (41 shorter events, 36.5 us)
Async XLA Ops:
  7.2 38.9 %all-gather.2.cloned.1.call-start = ((), (), s32[]{:S(2)}) async-start(), calls=%async_computation.4 | async-start | bytes 4718592 | tf_op jit(solution)/shard_map/all_gather | solution.py:111
  8.6 8.8 %collective-permute-start = (bf16[3,2,512]{2,1,0:T(2,128)(2,1)S(1)}, bf16[3,2,512]{2,1,0:T(2,128)(2,1)S(1)}, u32[]{:S(2)}, u32[]{:S(2)}) collective-permute-start(bf16[3,2,512]{2,1,0:T(2,128)(2,1)S(1)} %pad_maximum_fusion.15), channel_id=1, source_target_pairs={{0,8},{8,16},{16,24},{24,32},{32,40},{40,48},{48,56},{56,64},{64,7... | collective-permute-start | bytes 18440 | tf_op jit(solution)/shard_map/ppermute | solution.py:11
  46.0 7.2 %copy-start = (f32[1,256,512]{2,1,0:T(8,128)S(1)}, f32[1,256,512]{2,1,0:T(8,128)}, u32[]{:S(2)}) copy-start(f32[1,256,512]{2,1,0:T(8,128)} %slice_multiply_fusion.2) | copy-start | bytes 1572868
  46.0 7.2 %copy-start.1 = (f32[256,512]{1,0:T(8,128)S(1)}, f32[256,512]{1,0:T(8,128)}, u32[]{:S(2)}) copy-start(f32[256,512]{1,0:T(8,128)} %param.11) | copy-start | bytes 1572868
  56.1 46.5 %all-to-all-start = ((f32[3,1,256,512]{3,1,0,2:T(1,128)}), f32[3,1,256,512]{3,1,0,2:T(1,128)}, u32[]{:S(2)}, u32[]{:S(2)}) async-start(f32[3,1,256,512]{3,1,0,2:T(1,128)} %copy.56), calls=%async_computation | async-start | bytes 3145728 | tf_op jit(solution)/shard_map/all_to_all | solution.py:119
  497.6 44.2 %copy-start.2 = (f32[512]{0:T(512)S(1)}, f32[512]{0:T(512)}, u32[]{:S(2)}) copy-start(f32[512]{0:T(512)} %param.13) | copy-start | bytes 6148
  542.3 6.3 collective-permute-start.1
Sparse Core Ops, SparseCore 0:
  9.8 36.1 all-gather.1
where the time goes:
time: 707 us; the launch traced here: 702 us
  blocking collectives  477 us (67%)
  waiting for transfers between devices  67.8 us (10%)
  matrix products  66.2 us (9%)
  local copies, waits for them, and re-layouts  47.2 us (7%)
  starting transfers between devices  18.5 us (3%)
  between operations  14.6 us (2%)
  other arithmetic  11 us (2%)
    all_to_all x1, blocking collectives, forward_full(): lax.all_to_all(jnp.stack([second_real, second_imag], axis=1), 'ctx', spli...  145 us
    all_to_all x1, blocking collectives, inverse_full(): lax.all_to_all(jnp.stack([back_real, back_imag], axis=1), 'ctx', split_ax...  145 us
    psum x1, blocking collectives, per_device(): d_short, d_skip = lax.psum((short_terms, skip_term), 'ctx')  143 us
    dot_general x12, matrix products, mat_apply(): return jnp.einsum(form, table, data, precision=lax.Precision.HIGHEST)  59.1 us
    all_to_all x1, blocking collectives, per_device(): lax.all_to_all(result_real, 'ctx', split_axis=1, concat_axis=2, tiled=True)  43.2 us
    all_to_all x1, waiting for transfers between devices, per_device(): lax.all_to_all(signals[:, None], 'ctx', split_axis=2, concat_axis=1, tile...  36.3 us
    all_gather x1, waiting for transfers between devices, per_device(): lax.all_gather(d_out, 'ch', axis=1, tiled=True)  25.8 us
    all_to_all x3, local copies, waits for them, and re-layouts, inverse_full(): lax.all_to_all(jnp.stack([back_real, back_imag], axis=1), 'ctx', split_ax...  23.3 us
  transfers between devices with their start and end apart: 4, of which 4 were waited for; matrix products, arithmetic and copies ran while one was open for 1% of the time, Pallas kernels for 0%

commit v1 on v0

--- a/solution.py
+++ b/solution.py
@@ -64,8 +64,16 @@
     back_imag = mat_apply(fine_cos, spec_imag, "bk,smkc->smbc") + mat_apply(
         fine_sin, spec_real, "bk,smkc->smbc"
     )
-    returned = lax.all_to_all(
-        jnp.stack([back_real, back_imag], axis=1), "ctx", split_axis=3, concat_axis=2, tiled=True
+    returned = jnp.concatenate(
+        lax.all_to_all(
+            jnp.stack(
+                jnp.split(jnp.stack([back_real, back_imag], axis=1), lax.axis_size("ctx"), axis=3)
+            ),
+            "ctx",
+            0,
+            0,
+        ),
+        axis=2,
     )
     part_real = returned[:, 0]
     part_imag = returned[:, 1]

time: 707 us -> 691 us (0.977)
  local copies, waits for them, and re-layouts: 47.2 us -> 32.1 us
    all_to_all x3 -> x0, local copies, waits for them, and re-layouts: 23.3 us -> none  [inverse_full(): lax.all_to_all(jnp.stack([back_real, back_imag], axis=1), 'ctx', split_ax...]
    reshape x0 -> x2, local copies, waits for them, and re-layouts: none -> 18.7 us  [inverse_full(): jnp.concatenate(lax.all_to_all(jnp.stack(jnp.split(jnp.stack([back_real,...]
    another operation x1 -> x0, local copies, waits for them, and re-layouts: 10.3 us -> none  [inverse_full(): jnp.stack([back_real, back_imag], axis=1)]
where the time goes in v1:
time: 691 us; the launch traced here: 685 us
  blocking collectives  476 us (69%)
  waiting for transfers between devices  67.5 us (10%)
  matrix products  67.4 us (10%)
  local copies, waits for them, and re-layouts  32.1 us (5%)
  starting transfers between devices  18.8 us (3%)
  between operations  15 us (2%)
  other arithmetic  8.03 us (1%)
    all_to_all x1, blocking collectives, forward_full(): lax.all_to_all(jnp.stack([second_real, second_imag], axis=1), 'ctx', spli...  145 us
    all_to_all x1, blocking collectives, inverse_full(): lax.all_to_all(jnp.stack(jnp.split(jnp.stack([back_real, back_imag], axis...  145 us
    psum x1, blocking collectives, per_device(): d_short, d_skip = lax.psum((short_terms, skip_term), 'ctx')  143 us
    dot_general x12, matrix products, mat_apply(): return jnp.einsum(form, table, data, precision=lax.Precision.HIGHEST)  60.3 us
    all_to_all x1, blocking collectives, per_device(): lax.all_to_all(result_real, 'ctx', split_axis=1, concat_axis=2, tiled=True)  43 us
    all_to_all x1, waiting for transfers between devices, per_device(): lax.all_to_all(signals[:, None], 'ctx', split_axis=2, concat_axis=1, tile...  36 us
    all_gather x1, waiting for transfers between devices, per_device(): lax.all_gather(d_out, 'ch', axis=1, tiled=True)  25.8 us
    reshape x2, local copies, waits for them, and re-layouts, inverse_full(): jnp.concatenate(lax.all_to_all(jnp.stack(jnp.split(jnp.stack([back_real,...  18.7 us
  transfers between devices with their start and end apart: 4, of which 4 were waited for; matrix products, arithmetic and copies ran while one was open for 1% of the time, Pallas kernels for 0%

profile of v1, /device:TPU:128, one launch (start us, length us, event | category | flops | bytes accessed | tf_op | source)
XLA Modules:
  0.0 685.3 jit_solution(293283809649026237)
XLA Ops:
  13.0 4.5 collective-permute-done
  20.2 25.8 %all-gather.2.cloned.1.call-done = bf16[256,8192]{1,0:T(8,128)(2,1)} async-done(((bf16[256,1024]{1,0:T(8,128)(2,1)}), bf16[256,8192]{1,0:T(8,128)(2,1)}) %all-gather.2.cloned.1.call-update) | async-done | bytes 4194320 | tf_op jit(solution)/shard_map/all_gather | solution.py:119
  46.0 7.1 %convolution_convert_fusion = bf16[256,512]{1,0:T(8,128)(2,1)S(1)} fusion(bf16[256,8192]{1,0:T(8,128)(2,1)} %all-gather.2.cloned.1.call-done, bf16[512,8192]{1,0:T(8,128)(2,1)} %param.14), kind=kOutput, calls=%fused_computation.120 | convolution fusion | flops 2147614720 | bytes 12845056 | tf_op jit(solution)/shard_map/dot_general | solution.py:118
  56.1 10.3 %all-to-all-start = ((f32[3,1,256,512]{3,1,0,2:T(1,128)}), f32[3,1,256,512]{3,1,0,2:T(1,128)}, u32[]{:S(2)}, u32[]{:S(2)}) async-start(f32[3,1,256,512]{3,1,0,2:T(1,128)} %copy.67), calls=%async_computation | async-start | bytes 3145728 | tf_op jit(solution)/shard_map/all_to_all | solution.py:127
  66.6 36.0 %all-to-all-done = f32[3,1,256,512]{3,1,0,2:T(1,128)} async-done(((f32[3,1,256,512]{3,1,0,2:T(1,128)}), f32[3,1,256,512]{3,1,0,2:T(1,128)}, u32[]{:S(2)}, u32[]{:S(2)}) %all-to-all-start) | async-done | bytes 1572896 | tf_op jit(solution)/shard_map/all_to_all | solution.py:127
  104.2 4.0 fusion.29
  108.1 5.0 fusion.1
  118.2 145.3 %all_to_all.44 = f32[3,2,64,8,512]{4,3,0,1,2:T(8,128)S(1)} all-to-all(f32[3,2,64,8,512]{4,3,0,1,2:T(8,128)S(1)} %copy.71), channel_id=1, replica_groups=mesh['ctx'=32,'ch'=8] {'ctx'}, dimensions={2} | all-to-all | bytes 12582912 | tf_op jit(solution)/shard_map/all_to_all | solution.py:37
  264.5 6.3 fusion.12
  270.8 6.7 fusion.13
  277.5 6.3 subtract_bitcast_fusion.1
  283.8 6.5 add_bitcast_fusion.1
  291.2 4.1 fusion.16
  295.3 4.1 fusion.17
  299.4 4.1 add_bitcast_fusion
  303.5 4.3 subtract_bitcast_fusion
  308.6 144.8 %all_to_all.45 = f32[32,3,2,2,8,512]{5,4,3,1,2,0:T(8,128)} all-to-all(f32[32,3,2,2,8,512]{5,4,3,1,2,0:T(8,128)S(1)} %fusion.84), channel_id=1, replica_groups=mesh['ctx'=32,'ch'=8] {'ctx'}, dimensions={0} | all-to-all | bytes 12582912 | tf_op jit(solution)/shard_map/all_to_all | solution.py:68
  453.4 10.3 %copy.80 = f32[3,2,32,2,8,512]{5,3,2,4,0,1:T(2,128)} copy(f32[3,2,32,2,8,512]{5,4,3,0,1,2:T(8,128)} %bitcast.279) | data formatting | bytes 12582912 | tf_op jit(solution)/shard_map/reshape | solution.py:67
  463.7 8.5 %reshape.100 = f32[3,2,64,8,512]{4,2,3,0,1:T(8,128)} reshape(f32[3,2,32,2,8,512]{5,3,2,4,0,1:T(2,128)} %copy.80) | data formatting | bytes 12582912 | tf_op jit(solution)/shard_map/reshape | solution.py:67
  472.1 4.5 fusion.4
  476.6 4.6 multiply_bitcast_fusion
  482.1 43.0 %all_to_all.46 = f32[3,32,8,512]{3,2,0,1:T(8,128)S(1)} all-to-all(f32[3,32,8,512]{3,2,0,1:T(8,128)S(1)} %copy.81), channel_id=1, replica_groups=mesh['ctx'=32,'ch'=8] {'ctx'}, dimensions={1} | all-to-all | bytes 3145728 | tf_op jit(solution)/shard_map/all_to_all | solution.py:146
  525.6 5.0 collective-permute-start.1
  533.2 143.3 %all-reduce = (f32[3,3,512]{2,0,1:T(4,128)S(1)}, f32[512]{0:T(512)}) all-reduce(f32[3,3,512]{2,0,1:T(4,128)S(1)} %pad_maximum_fusion.14, f32[512]{0:T(512)S(1)} %get-tuple-element.46), channel_id=1, replica_groups=mesh['ctx'=32,'ch'=8] {'ctx'}, use_global_device_ids=true, to_apply=%region_3.4 | all-reduce | flops 5120 | bytes 40960 | tf_op jit(solution)/shard_map/psum | solution.py:168
  (70 shorter events, 26.1 us)
Async XLA Ops:
  7.2 38.9 %all-gather.2.cloned.1.call-start = ((), (), s32[]{:S(2)}) async-start(), calls=%async_computation.4 | async-start | bytes 4718592 | tf_op jit(solution)/shard_map/all_gather | solution.py:119
  8.6 8.8 %collective-permute-start = (bf16[3,2,512]{2,1,0:T(2,128)(2,1)S(1)}, bf16[3,2,512]{2,1,0:T(2,128)(2,1)S(1)}, u32[]{:S(2)}, u32[]{:S(2)}) collective-permute-start(bf16[3,2,512]{2,1,0:T(2,128)(2,1)S(1)} %pad_maximum_fusion.15), channel_id=1, source_target_pairs={{0,8},{8,16},{16,24},{24,32},{32,40},{40,48},{48,56},{56,64},{64,7... | collective-permute-start | bytes 18440 | tf_op jit(solution)/shard_map/ppermute | solution.py:11
  46.0 7.2 %copy-start = (f32[1,256,512]{2,1,0:T(8,128)S(1)}, f32[1,256,512]{2,1,0:T(8,128)}, u32[]{:S(2)}) copy-start(f32[1,256,512]{2,1,0:T(8,128)} %slice_multiply_fusion.2) | copy-start | bytes 1572868
  46.0 7.2 %copy-start.1 = (f32[256,512]{1,0:T(8,128)S(1)}, f32[256,512]{1,0:T(8,128)}, u32[]{:S(2)}) copy-start(f32[256,512]{1,0:T(8,128)} %param.11) | copy-start | bytes 1572868
  56.1 46.5 %all-to-all-start = ((f32[3,1,256,512]{3,1,0,2:T(1,128)}), f32[3,1,256,512]{3,1,0,2:T(1,128)}, u32[]{:S(2)}, u32[]{:S(2)}) async-start(f32[3,1,256,512]{3,1,0,2:T(1,128)} %copy.67), calls=%async_computation | async-start | bytes 3145728 | tf_op jit(solution)/shard_map/all_to_all | solution.py:127
  481.2 43.9 %copy-start.2 = (f32[512]{0:T(512)S(1)}, f32[512]{0:T(512)}, u32[]{:S(2)}) copy-start(f32[512]{0:T(512)} %param.13) | copy-start | bytes 6148
  525.6 6.4 collective-permute-start.1
Sparse Core Ops, SparseCore 0:
  9.8 36.1 all-gather.1
